TPU v7x, 32 devices: a whole 2x2x4 slice. The times are simulated.
32 devices in a mesh: row: 4 (over y, core), col: 8 (over z, x).
Axes of the slice: x: 2, y: 2, z: 4, core: 2. Of those that a mesh axis runs over, the one named last changes fastest.
Arguments:
- block_values: bfloat16 [512, 8, 128, 128], P(('row', 'col')), as said below
- block_cols: int32 [512, 8], P(('row', 'col')), may hold values from 0 to 511, as said below
- block_present: int32 [512, 8], P(('row', 'col')), may hold values from 0 to 1, as said below
Outputs:
- sign_step: bfloat16 [512, 8, 128, 128], P('row', 'col')
Inputs may be any that keep to these rules, and one draw needn't show every extreme that they name: block_cols[i, g] lies in [g * 64, (g + 1) * 64); the slot whose range holds i names i itself. The slots are paired symmetrically: if block_cols[i, g] = j then block_cols[j, i * 8 // 512] = i. `block_present`: symmetric under the pairing of block_cols; the slot of the diagonal block is always 1. `block_values`: zero where block_present is 0; the paired slot of (i, g) holds the transpose of block (i, g), so H is symmetric.
All inputs are finite; a program needn't handle non-finite values.
Results may differ from a plain program's by a relative error of at most 0.0013.
Values may be sent and summed in bfloat16 or wider, within the bound.
A program may use at most 256 MiB of HBM per device.

v0:
```python
import jax
import jax.numpy as jnp
from jax import lax
from jax.sharding import PartitionSpec as P


def broadcast(value, axis, source):
    kept = jnp.where(lax.axis_index(axis) == source, value, 0).astype(value.dtype)
    return lax.psum(kept, axis)


def body(block_values, block_cols, block_present):
    row_count = lax.axis_size("row")
    col_count = lax.axis_size("col")
    per_device = block_values.shape[0]
    slot_count = block_values.shape[1]
    block_width = block_values.shape[2]
    panel_rows = per_device * col_count
    block_total = panel_rows * row_count
    col_width = block_total // col_count
    col_here = lax.axis_index("col")
    slot_here = col_here * slot_count // col_count
    first_col = col_here * col_width
    weighted = block_values * block_present[:, :, None, None].astype(block_values.dtype)
    panel_v, panel_c, panel_p = (
        lax.all_gather(weighted, "col", axis=0, tiled=True),
        lax.all_gather(block_cols, "col", axis=0, tiled=True),
        lax.all_gather(block_present, "col", axis=0, tiled=True),
    )
    share_count = col_count // row_count
    offset = col_here % share_count * col_width
    portions = (
        lax.dynamic_slice_in_dim(panel_v, offset, col_width, 0),
        lax.dynamic_slice_in_dim(panel_c, offset, col_width, 0),
    )
    column_v, column_c = (
        broadcast(portions[0], "row", col_here // share_count),
        broadcast(portions[1], "row", col_here // share_count),
    )
    target = lax.dynamic_index_in_dim(panel_c, slot_here, 1, keepdims=False)
    wanted = lax.dynamic_index_in_dim(panel_p, slot_here, 1, keepdims=False)
    inside = (target >= first_col) & (target < first_col + col_width) & (wanted > 0)
    live_rows = jnp.where(inside, 1.0, 0.0).astype(jnp.float32)
    local_cols = jnp.clip(target - first_col, 0, col_width - 1)
    chosen_v = jnp.take(column_v, local_cols, axis=0)
    chosen_c = jnp.take(column_c, local_cols, axis=0)
    matched = chosen_v * (chosen_c == panel_c).astype(chosen_v.dtype)[:, :, None, None]
    square_sum = jnp.einsum("igab,igcb->iac", panel_v, matched, preferred_element_type=jnp.float32)
    square = (square_sum / 1600.0 * live_rows[:, None, None]).astype(jnp.bfloat16)
    arrived = lax.all_to_all(square, "col", split_axis=0, concat_axis=0, tiled=True)
    arrived = arrived.reshape(
        slot_count, col_count // slot_count, per_device, block_width, block_width
    )
    owned_square = jnp.sum(arrived.astype(jnp.float32), axis=1).astype(jnp.bfloat16)
    own_slot = lax.dynamic_index_in_dim(panel_v, slot_here, 1, keepdims=False)
    square_rows = lax.all_gather(owned_square, "col", axis=1, tiled=True)
    product_sum = jnp.einsum(
        "giab,igcb->iac", square_rows, matched, preferred_element_type=jnp.float32
    )
    own_rows = own_slot.astype(jnp.float32)
    result_rows = ((1.5 * own_rows - 0.5 * product_sum) * live_rows[:, None, None]).astype(
        jnp.bfloat16
    )
    return result_rows[:, None, :, :]


def solution(mesh):
    return jax.shard_map(
        body,
        mesh=mesh,
        in_specs=(
            P(("row", "col"), None, None, None),
            P(("row", "col"), None),
            P(("row", "col"), None),
        ),
        out_specs=P("row", "col", None, None),
        check_vma=False,
    )
```

profile of v0, /device:TPU:15, one launch (start us, length us, event | category | flops | bytes accessed | tf_op | source)
XLA Modules:
  0.0 1766.1 jit_solution(15543690502624117305)
XLA Ops:
  6.5 0.0 all-gather.5.cloned.1.call-start
  6.5 0.7 convert_element_type.24
  7.2 0.1 copy.14
  7.3 4.5 broadcast_multiply_fusion
  11.9 0.0 all-gather.5.cloned.1.call-update
  11.9 0.0 all-reduce.2.cloned.1.call-start
  12.0 638.0 %all-gather.5.cloned.1.call-done = bf16[128,8,128,128]{3,2,1,0:T(8,128)(2,1)} async-done(((bf16[16,8,128,128]{3,2,1,0:T(8,128)(2,1)}), bf16[128,8,128,128]{3,2,1,0:T(8,128)(2,1)}) %all-gather.5.cloned.1.call-update) | async-done | bytes 33554448 | tf_op jit(solution)/shard_map/all_gather | solution.py:26
  650.0 13.7 dynamic-slice_select_fusion
  663.7 0.0 copy-start.1
  663.7 0.0 copy-start
  663.7 0.0 all-reduce.2.cloned.1.call-update
  663.7 0.0 all-gather.7.cloned.1.call-start
  663.8 0.6 copy-done.1
  664.4 22.4 %all-gather = s32[8,16,8]{1,2,0:T(8,128)S(1)} all-gather(s32[1,16,8]{1,2,0:T(8,128)S(1)} %bitcast.41), channel_id=1, replica_groups=mesh['row'=4,'col'=8] {'col'}, dimensions={0}, use_global_device_ids=true | all-gather | bytes 4608 | tf_op jit(solution)/shard_map/all_gather | solution.py:27
  686.8 0.1 copy.16
  686.9 0.0 copy-done
  686.9 24.0 %all-gather.1 = s32[8,16,8]{1,2,0:T(8,128)S(1)} all-gather(s32[1,16,8]{1,2,0:T(8,128)S(1)} %bitcast.40), channel_id=1, replica_groups=mesh['row'=4,'col'=8] {'col'}, dimensions={0}, use_global_device_ids=true | all-gather | bytes 4608 | tf_op jit(solution)/shard_map/all_gather | solution.py:28
  710.9 0.1 copy.17
  710.9 22.8 %psum.15 = s32[64,8]{1,0:T(8,128)S(1)} all-reduce(s32[64,8]{1,0:T(8,128)S(1)} %dynamic-slice_select_fusion.1), channel_id=1, replica_groups=mesh['row'=4,'col'=8] {'row'}, use_global_device_ids=true, to_apply=%region_1.2 | all-reduce | flops 512 | bytes 4096 | tf_op jit(solution)/shard_map/psum | solution.py:9
  733.8 0.2 fusion.9
  733.9 0.7 gather_fusion.1
  734.6 0.2 select_reduce_fusion
  734.8 0.2 and_reduce_fusion
  735.0 0.1 fusion.7
  735.1 217.8 %all-reduce.2.cloned.1.call-done = bf16[64,8,128,128]{3,2,1,0:T(8,128)(2,1)} async-done(((bf16[64,8,128,128]{3,2,1,0:T(8,128)(2,1)}), bf16[64,8,128,128]{3,2,1,0:T(8,128)(2,1)}) %all-reduce.2.cloned.1.call-update) | async-done | bytes 16777232 | tf_op jit(solution)/shard_map/psum | solution.py:9
  952.9 18.7 %gather_fusion = bf16[128,8,128,128]{3,2,1,0:T(8,128)(2,1)} fusion(bf16[64,8,128,128]{3,2,1,0:T(8,128)(2,1)} %all-reduce.2.cloned.1.call-done, s32[1024]{0:T(1024)S(1)} %pad_clamp_fusion), kind=kCustom, calls=%fused_computation | custom fusion | bytes 67109376 | tf_op jit(solution)/shard_map/jit(_take)/gather | solution.py:45
  971.6 25.0 %fusion.5 = bf16[128,128,128]{2,1,0:T(8,128)(2,1)} fusion(f32[128]{0:T(128)S(1)} %broadcast_multiply_fusion.1, bf16[128,8,128,128]{3,2,1,0:T(8,128)(2,1)} %all-gather.5.cloned.1.call-done, bf16[128,8,128,128]{3,2,1,0:T(8,128)(2,1)} %gather_fusion, pred[128]{0:T(512)(128)(4,1)S(1)} %and_reduce_fusion, bf16[128,8]{1,0:T(8,128)(2,1)S(1)} %fusion.7), kind=kOutput, calls=%fused_computation.11 | convolution fusion | flops 4332716032 | bytes 71305856 | tf_op jit(solution)/shard_map/igab,igcb->iac/dot_general | solution.py:48
  996.6 95.8 %all_to_all.5 = bf16[128,128,128]{2,1,0:T(8,128)(2,1)S(1)} all-to-all(bf16[128,128,128]{2,1,0:T(8,128)(2,1)} %fusion.5), channel_id=1, replica_groups=mesh['row'=4,'col'=8] {'col'}, dimensions={0} | all-to-all | bytes 8388608 | tf_op jit(solution)/shard_map/all_to_all | solution.py:50
  1092.4 2.3 copy.18
  1094.7 0.0 all-gather.7.cloned.1.call-update
  1094.7 638.9 %all-gather.7.cloned.1.call-done = bf16[8,128,128,128]{3,2,0,1:T(8,128)(2,1)} async-done(((bf16[8,16,128,128]{3,2,0,1:T(8,128)(2,1)}), bf16[8,128,128,128]{3,2,0,1:T(8,128)(2,1)}) %all-gather.7.cloned.1.call-update) | async-done | bytes 33554448 | tf_op jit(solution)/shard_map/all_gather | solution.py:56
  1733.6 26.0 %fusion.6 = bf16[128,1,128,128]{3,2,1,0:T(8,128)(2,1)} fusion(f32[128]{0:T(128)S(1)} %select_reduce_fusion, bf16[128,8,128,128]{3,2,1,0:T(8,128)(2,1)} %all-gather.5.cloned.1.call-done, s32[]{:T(128)S(6)} %select_n.71, bf16[8,128,128,128]{3,2,0,1:T(8,128)(2,1)} %all-gather.7.cloned.1.call-done, bf16[128,8,128,128]{3,2,1,0:T(8,128)(2,1)} %gather_fusion, ...), kind=kOutput, calls=%fused_computation.12 | convolution fusion | flops 4341104640 | bytes 75500160 | tf_op jit(solution)/shard_map/giab,igcb->iac/dot_general | solution.py:57
  (3 shorter events, 0.0 us)
Async XLA Ops:
  6.5 643.4 %all-gather.5.cloned.1.call-start = ((), (), s32[]{:S(2)}) async-start(), calls=%async_computation.1 | async-start | bytes 37748736 | tf_op jit(solution)/shard_map/all_gather | solution.py:26
  11.9 941.0 %all-reduce.2.cloned.1.call-start = ((), (), s32[]{:S(2)}) async-start(), calls=%async_computation.2 | async-start | bytes 33554432 | tf_op jit(solution)/shard_map/psum | solution.py:9
  663.7 0.7 copy-start.1
  663.7 23.2 %copy-start = (s32[16,8]{0,1:T(8,128)S(1)}, s32[16,8]{0,1:T(8,128)}, u32[]{:S(2)}) copy-start(s32[16,8]{0,1:T(8,128)} %param.5) | copy-start | bytes 1540
  663.7 1069.9 %all-gather.7.cloned.1.call-start = ((), (), s32[]{:S(2)}) async-start(), calls=%async_computation.3 | async-start | bytes 37748736 | tf_op jit(solution)/shard_map/all_gather | solution.py:56
Sparse Core Ops, SparseCore 0:
  12.0 637.9 all-gather.4
  663.9 288.9 all-reduce.1
  1094.9 638.7 all-gather.6
where the time goes:
time: 1770 us
  waiting for transfers between devices  1490 us (84%)
  blocking collectives  165 us (9%)
  matrix products  51 us (3%)
  local copies, waits for them, and re-layouts  22.5 us (1%)
  other arithmetic  19.6 us (1%)
    all_gather x1, waiting for transfers between devices, body(): square_rows = lax.all_gather(owned_square, 'col', axis=1, tiled=True)  639 us
    all_gather x1, waiting for transfers between devices, body(): lax.all_gather(weighted, 'col', axis=0, tiled=True)  638 us
    psum x1, waiting for transfers between devices, broadcast(): return lax.psum(kept, axis)  218 us
    all_to_all x1, blocking collectives, body(): lax.all_to_all(square, 'col', split_axis=0, concat_axis=0, tiled=True)  95.8 us
  transfers between devices with their start and end apart: 3, of which 3 were waited for; matrix products, arithmetic and copies ran while one was open for 0% of the time, Pallas kernels for 0%

commit v1 on v0

v1 whole, which is shorter than its diff:
```python
import functools

import jax
import jax.numpy as jnp
from jax import lax
from jax.experimental import pallas as pl
from jax.experimental.pallas import tpu as pltpu
from jax.sharding import PartitionSpec as P

MESH = pl.DeviceIdType.MESH
SLOTS = 8
SENT = 5


def sent_slot(u, index):
    tile, parity = u // 2, u % 2
    if index < 4:
        return (2 * tile + index) % SLOTS
    return u + 4 if tile < 2 else 2 * (tile - 2) + 1 - parity


def gather_kernel(sizes, own_ref, all_ref, send_sem, recv_sem, local_sem):
    nx, ny, nz = sizes
    row, col = lax.axis_index("row"), lax.axis_index("col")
    y, core = row // 2, row % 2
    z, x = col // nx, col % nx
    rows = own_ref.shape[0]
    half = rows // 2
    col_count = nx * nz

    def place(px, py, pz, pcore):
        return (py * 2 + pcore, pz * nx + px)

    def index(where):
        return where[0] * col_count + where[1]

    def x_peer(k):
        return lax.rem(x + k, nx)

    def y_peer(k):
        return lax.rem(y + k, ny)

    def z_peer(k):
        return lax.rem(z + k, nz)

    here = place(x, y, z, core)
    sibling = place(x, y, z, 1 - core)
    x_places = [place(x_peer(k), y, z, core) for k in range(1, nx)]
    y_places = [place(x, y_peer(k), z, core) for k in range(1, ny)]
    z_places = [place(x, y, z_peer(k), core) for k in range(1, nz)]
    partners = x_places + y_places + z_places + [sibling]

    barrier = pltpu.get_barrier_semaphore()
    for partner in partners:
        pl.semaphore_signal(barrier, inc=1, device_id=partner, device_id_type=MESH)
    pl.semaphore_wait(barrier, len(partners))

    sends = []

    def window(origin, part):
        return all_ref.at[pl.ds(index(origin) * rows + part * half, half)]

    def send(origin, part, target, own=False):
        source = own_ref.at[pl.ds(part * half, half)] if own else window(origin, part)
        copy = pltpu.make_async_remote_copy(
            src_ref=source,
            dst_ref=window(origin, part),
            send_sem=send_sem.at[len(sends)],
            recv_sem=recv_sem.at[index(origin) * 2 + part],
            device_id=target,
            device_id_type=MESH,
        )
        copy.start()
        sends.append(copy)

    def arrived(origin, part):
        pltpu.make_async_copy(
            window(origin, part), window(origin, part), recv_sem.at[index(origin) * 2 + part]
        ).wait()

    keep = pltpu.make_async_copy(own_ref, all_ref.at[pl.ds(index(here) * rows, rows)], local_sem)
    keep.start()

    def first(k):
        origin = place(x, y, z_peer(k), core)
        if k > 0:
            for part in range(2):
                arrived(origin, part)
        own = k == 0
        for target in x_places:
            send(origin, 0, target, own)
        for target in y_places:
            send(origin, 1, target, own)
        if own:
            for target in z_places:
                for part in range(2):
                    send(origin, part, target, own)
        for target in x_places:
            send(origin, 1, target, own)
        for target in y_places:
            send(origin, 0, target, own)
        for part in range(2):
            send(origin, part, sibling, own)

    def second(k):
        for n in range(1, nx):
            origin = place(x_peer(n), y, z_peer(k), core)
            arrived(origin, 0)
            for target in y_places:
                send(origin, 0, target)
            send(origin, 0, sibling)
        for n in range(1, ny):
            origin = place(x, y_peer(n), z_peer(k), core)
            arrived(origin, 1)
            for target in x_places:
                send(origin, 1, target)
            send(origin, 1, sibling)

    def third(k):
        for n in range(1, ny):
            origin = place(x, y_peer(n), z_peer(k), core)
            arrived(origin, 0)
            send(origin, 0, sibling)
        for n in range(1, nx):
            origin = place(x_peer(n), y, z_peer(k), core)
            arrived(origin, 1)
            send(origin, 1, sibling)
        for n in range(1, nx):
            for m in range(1, ny):
                origin = place(x_peer(n), y_peer(m), z_peer(k), core)
                for part in range(2):
                    arrived(origin, part)
                    send(origin, part, sibling)

    for k in range(nz + 2):
        if k < nz:
            first(k)
        if 0 <= k - 1 < nz:
            second(k - 1)
        if 0 <= k - 2 < nz:
            third(k - 2)

    for n in range(nx):
        for m in range(ny):
            for k in range(nz):
                origin = place(x_peer(n), y_peer(m), z_peer(k), 1 - core)
                for part in range(2):
                    arrived(origin, part)
    keep.wait()
    for copy in sends:
        copy.wait_send()


def send_count(sizes):
    nx, ny, nz = sizes
    plane = 2 * (nx - 1) + 2 * (ny - 1) + 2 * (nx - 1) * (ny - 1)
    return nz * plane + 2 * (nz - 1) + 2 * nx * ny * nz


def gather_rows(own, sizes, total):
    shape = (total,) + own.shape[1:]
    return pl.pallas_call(
        functools.partial(gather_kernel, sizes),
        out_shape=jax.ShapeDtypeStruct(shape, own.dtype),
        in_specs=[pl.BlockSpec(memory_space=pl.ANY)],
        out_specs=pl.BlockSpec(memory_space=pl.ANY),
        scratch_shapes=[
            pltpu.SemaphoreType.DMA((send_count(sizes),)),
            pltpu.SemaphoreType.DMA((2 * total // own.shape[0],)),
            pltpu.SemaphoreType.DMA,
        ],
        compiler_params=pltpu.CompilerParams(collective_id=0, has_side_effects=True),
        name="gather_rows",
    )(own)


def stored_tiles():
    tiles = []
    for t in range(4):
        u = 2 * t
        tiles.append((t, t, [[(u, 0), (u, 1)], [(u + 1, 0), (u + 1, 1)]]))
    for t in range(4):
        u = 2 * t
        tiles.append((t, (t + 1) % 4, [[(u, 2), (u, 3)], [(u + 1, 2), (u + 1, 3)]]))
    for t in range(2):
        u, v = 2 * t, 2 * t + 4
        tiles.append((t, t + 2, [[(u, 4), (v + 1, 4)], [(v, 4), (u + 1, 4)]]))
    return tiles


TILES = stored_tiles()


def sign_kernel(cols_ref, flags_ref, present_ref, home_ref, live_ref, slot_ref, *refs):
    rows = refs[:SLOTS]
    out_ref, left_ref, tile_ref, square_ref, total_ref = refs[SLOTS:]
    width = out_ref.shape[-1]
    i = pl.program_id(0)
    home = home_ref[i]
    slot = slot_ref[0]

    for a in range(SLOTS):

        @pl.when(home == a)
        def _(a=a):
            tile, parity = a // 2, a % 2
            for g in range(SLOTS):
                other, q = g // 2, g % 2
                if other == tile:
                    block = rows[a][0, q]
                elif other == (tile + 1) % 4:
                    block = rows[a][0, 2 + q]
                elif other == (tile - 1) % 4:
                    block = rows[g][0, 2 + parity].T
                else:
                    block = rows[a][0, 4] if sent_slot(a, 4) == g else rows[g][0, 4]
                    if tile >= 2:
                        block = block.T
                left_ref[g] = block

    for n, (_, _, blocks) in enumerate(TILES):
        for p in range(2):
            for q in range(2):
                u, index = blocks[p][q]
                kept = flags_ref[(i * SLOTS + u) * SENT + index] > 0
                block = rows[u][0, index]
                tile_ref[n, pl.ds(p * width, width), pl.ds(q * width, width)] = jnp.where(
                    kept, block, jnp.zeros_like(block)
                )

    def plain(left, n):
        return jnp.dot(left, tile_ref[n], preferred_element_type=jnp.float32)

    def turned(left, n):
        return lax.dot_general(
            left, tile_ref[n], (((1,), (1,)), ((), ())), preferred_element_type=jnp.float32
        )

    def column(left, t):
        total = None
        for n, (first, second, _) in enumerate(TILES):
            term = None
            if second == t:
                term = plain(left(first), n)
            elif first == t:
                term = turned(left(second), n)
            if term is not None:
                total = term if total is None else total + term
        return total

    def left_tile(t):
        return jnp.concatenate([left_ref[2 * t], left_ref[2 * t + 1]], axis=1)

    for t in range(4):
        product = column(left_tile, t) * (1.0 / 1600.0)
        for q in range(2):
            kept = present_ref[i * SLOTS + 2 * t + q] > 0
            part = product[:, q * width : (q + 1) * width]
            square_ref[2 * t + q] = jnp.where(kept, part, 0.0).astype(square_ref.dtype)

    def square_tile(t):
        return jnp.concatenate([square_ref[2 * t], square_ref[2 * t + 1]], axis=1)

    for t in range(4):

        @pl.when(slot // 2 == t)
        def _(t=t):
            product = column(square_tile, t)
            total_ref[0] = product[:, :width]
            total_ref[1] = product[:, width:]

    updated = 1.5 * left_ref[slot].astype(jnp.float32) - 0.5 * total_ref[slot % 2]
    out_ref[0, 0] = jnp.where(live_ref[i] > 0, updated, 0.0).astype(out_ref.dtype)


def sign_rows(gathered, cols, flags, present, home, live, slot):
    count = cols.shape[0]
    width = gathered.shape[-1]

    def row_spec(u):
        return pl.BlockSpec(
            (1, SENT, width, width), lambda i, cols, *rest, u=u: (cols[i * SLOTS + u], 0, 0, 0)
        )

    return pl.pallas_call(
        sign_kernel,
        grid_spec=pltpu.PrefetchScalarGridSpec(
            num_scalar_prefetch=6,
            grid=(count,),
            in_specs=[row_spec(u) for u in range(SLOTS)],
            out_specs=pl.BlockSpec((1, 1, width, width), lambda i, *rest: (i, 0, 0, 0)),
            scratch_shapes=[
                pltpu.VMEM((SLOTS, width, width), gathered.dtype),
                pltpu.VMEM((len(TILES), 2 * width, 2 * width), gathered.dtype),
                pltpu.VMEM((SLOTS, width, width), gathered.dtype),
                pltpu.VMEM((2, width, width), jnp.float32),
            ],
        ),
        out_shape=jax.ShapeDtypeStruct((count, 1, width, width), gathered.dtype),
        compiler_params=pltpu.CompilerParams(vmem_limit_bytes=40 * 2**20),
        cost_estimate=pl.CostEstimate(
            flops=count * 10 * SLOTS * 2 * SLOTS * width**3 // SLOTS,
            bytes_accessed=count * SLOTS * SENT * width * width * 2,
            transcendentals=0,
        ),
        name="sign_rows",
    )(cols.reshape(-1), flags.reshape(-1), present.reshape(-1), home, live, slot, *[gathered] * SLOTS)


def body(sizes, block_values, block_cols, block_present):
    row_count, col_count = lax.axis_size("row"), lax.axis_size("col")
    per_device = block_values.shape[0]
    panel_rows = per_device * col_count
    block_total = panel_rows * row_count
    range_width = block_total // SLOTS
    col_width = block_total // col_count
    row_here, col_here = lax.axis_index("row"), lax.axis_index("col")
    slot_here = col_here * SLOTS // col_count
    device = row_here * col_count + col_here

    codes = lax.all_gather(block_cols * 2 + block_present, ("row", "col"), axis=0, tiled=True)
    all_cols = codes // 2

    slots = jnp.array([[sent_slot(u, k) for k in range(SENT)] for u in range(SLOTS)], jnp.int32)
    range_here = device * per_device // range_width
    mine = slots[range_here]
    parts = [
        lax.dynamic_index_in_dim(block_values, mine[k], 1, keepdims=False) for k in range(SENT)
    ]
    parts[-1] = jnp.where(range_here >= SLOTS // 2, jnp.swapaxes(parts[-1], 1, 2), parts[-1])
    own = jnp.stack(parts, axis=1)
    gathered = gather_rows(own, sizes, block_total)

    first_row = row_here * panel_rows
    panel = lax.dynamic_slice_in_dim(codes, first_row, panel_rows, 0)
    cols, present = panel // 2, panel % 2
    neighbour_cols = jnp.take(all_cols, cols, axis=0)
    same = neighbour_cols == cols[:, None, :]
    flags = jnp.stack(
        [
            jnp.stack([same[:, u, sent_slot(u, k)] for k in range(SENT)], axis=1)
            for u in range(SLOTS)
        ],
        axis=1,
    ).astype(jnp.int32)
    target = lax.dynamic_index_in_dim(cols, slot_here, 1, keepdims=False)
    wanted = lax.dynamic_index_in_dim(present, slot_here, 1, keepdims=False)
    live = ((target // col_width == col_here) & (wanted > 0)).astype(jnp.int32)
    home = ((first_row + jnp.arange(panel_rows, dtype=jnp.int32)) // range_width).astype(jnp.int32)
    slot = jnp.reshape(slot_here, (1,)).astype(jnp.int32)
    return sign_rows(gathered, cols, flags, present, home, live, slot)


def solution(mesh):
    rows, cols = mesh.shape["row"], mesh.shape["col"]
    nz = 4 if cols % 4 == 0 else 1
    sizes = (cols // nz, rows // 2, nz)
    return jax.shard_map(
        functools.partial(body, sizes),
        mesh=mesh,
        in_specs=(
            P(("row", "col"), None, None, None),
            P(("row", "col"), None),
            P(("row", "col"), None),
        ),
        out_specs=P("row", "col", None, None),
        check_vma=False,
    )
```

time: 1770 us -> 785 us (0.44)
  waiting for transfers between devices: 1490 us -> 0 us
  Pallas kernels: 0 us -> 698 us
  blocking collectives: 165 us -> 56.5 us
  matrix products: 51 us -> 0 us
    all_gather x2 -> x0, waiting for transfers between devices: 1280 us -> none  [the longest x1 639 us: body(): square_rows = lax.all_gather(owned_square, 'col', axis=1, tiled=True)]
    pallas_call x0 -> x2, Pallas kernels: none -> 698 us  [the longest x1 524 us: gather_rows(): pl.pallas_call(functools.partial(gather_kernel, sizes), out_shape=jax.Sha...]
    psum x1 -> x0, waiting for transfers between devices: 218 us -> none  [broadcast(): return lax.psum(kept, axis)]
    all_to_all x1 -> x0, blocking collectives: 95.8 us -> none  [body(): lax.all_to_all(square, 'col', split_axis=0, concat_axis=0, tiled=True)]
    dot_general x2 -> x0, matrix products: 51 us -> none  [the longest x1 26 us: body(): jnp.einsum('giab,igcb->iac', square_rows, matched, preferred_element_type...]
    psum x1 -> x0, blocking collectives: 22.8 us -> none  [broadcast(): return lax.psum(kept, axis)]
    all_gather x2 -> x1, blocking collectives: 46.4 us -> 56.5 us  [body(): lax.all_gather(block_cols * 2 + block_present, ('row', 'col'), axis=0, ti...]
  transfers between devices with their start and end apart: 3 -> 0, of which waited for: 3 -> 0; matrix products, arithmetic and copies ran while one was open for 0% -> 0% of each run, Pallas kernels for 0% -> 0%
where the time goes in v1:
time: 785 us; the launch traced here: 781 us
  Pallas kernels  698 us (89%)
  blocking collectives  56.5 us (7%)
  local copies, waits for them, and re-layouts  14.5 us (2%)
  between operations  9.64 us (1%)
    pallas_call x1, Pallas kernels, gather_rows(): pl.pallas_call(functools.partial(gather_kernel, sizes), out_shape=jax.Sha...  524 us
    pallas_call x1, Pallas kernels, sign_rows(): pl.pallas_call(sign_kernel, grid_spec=pltpu.PrefetchScalarGridSpec(num_sc...  175 us
    all_gather x1, blocking collectives, body(): lax.all_gather(block_cols * 2 + block_present, ('row', 'col'), axis=0, ti...  56.5 us

profile of v1, /device:TPU:15, one launch (start us, length us, event | category | flops | bytes accessed | tf_op | source)
XLA Modules:
  0.0 781.3 jit_solution(1754178390166413111)
XLA Ops:
  0.0 0.7 constant_dynamic-slice_fusion
  0.7 0.7 fusion.7
  10.8 0.7 add_bitcast_fusion
  11.5 56.5 %all-gather = s32[32,16,8]{1,2,0:T(8,128)S(1)} all-gather(s32[1,16,8]{1,2,0:T(8,128)S(1)} %add_bitcast_fusion), channel_id=1, replica_groups=mesh['row'=4,'col'=8] {'row','col'}, dimensions={0}, use_global_device_ids=true | all-gather | bytes 16896 | tf_op jit(solution)/shard_map/all_gather | solution.py:321
  68.1 0.1 reshape.46
  68.3 0.1 copy.36
  68.4 0.1 reshape.37
  68.5 0.1 copy.47
  68.6 0.1 reshape.32.present_ref
  68.7 0.1 copy.31
  68.8 0.1 reshape.31.cols_ref
  68.9 0.1 copy.32
  69.0 0.1 add_select_fusion
  69.2 2.8 gather_fusion
  72.0 0.2 copy.37
  72.7 0.1 stack.77
  72.7 0.3 copy.46
  73.0 0.3 reshape.34.flags_ref
  73.3 1.1 dynamic-slice_dynamic-update-slice_fusion.3
  74.4 1.1 dynamic-slice_dynamic-update-slice_fusion.2
  75.5 2.1 dynamic-slice_bitcast_fusion
  77.7 1.3 copy.48
  79.0 1.1 dynamic-slice_dynamic-update-slice_fusion
  80.1 1.3 bitcast_dynamic-update-slice_fusion.own_ref
  81.4 0.0 copy-start
  81.4 1.5 copy-done
  82.9 523.8 %gather_rows.1.refs_0_.refs_1_.refs_2_.refs_3_.refs_4_.refs_5_.refs_6_.refs_7_ = bf16[512,5,128,128]{3,2,1,0:T(8,128)(2,1)} custom-call(bf16[16,5,128,128]{3,2,1,0:T(8,128)(2,1)} %copy-done), custom_call_target="tpu_custom_call" | custom-call | tf_op jit(solution)/shard_map/gather_rows/pallas_call | solution.py:162
  606.7 174.5 %sign_rows.1 = bf16[128,1,128,128]{3,2,1,0:T(8,128)(2,1)} custom-call(s32[1024]{0:T(1024)S(1)} %reshape.31.cols_ref, s32[5120]{0:T(1024)S(1)} %reshape.34.flags_ref, s32[1024]{0:T(1024)S(1)} %reshape.32.present_ref, s32[128]{0:T(128)S(1)} %and_select_fusion.1.home_ref, s32[128]{0:T(128)S(1)} %fusion.4.live_ref, s32[1]{0:T(128)} %bitcast.52.slot_ref, ...), custom_call_target="tpu_custom_call" | custom-call | flops 42949672960 | bytes 167772160 | tf_op jit(solution)/shard_map/sign_rows/pallas_call | solution.py:285
  (28 shorter events, 0.5 us)
Async XLA Ops:
  81.4 1.5 copy-start

commit v2 on v1

--- a/solution.py
+++ b/solution.py
@@ -19,7 +19,9 @@
     return u + 4 if tile < 2 else 2 * (tile - 2) + 1 - parity
 
 
-def gather_kernel(sizes, own_ref, all_ref, send_sem, recv_sem, local_sem):
+def gather_kernel(
+    sizes, own_ref, own_codes_ref, all_ref, all_codes_ref, send_sem, recv_sem, local_sem
+):
     nx, ny, nz = sizes
     row, col = lax.axis_index("row"), lax.axis_index("col")
     y, core = row // 2, row % 2
@@ -40,15 +42,22 @@
     def y_peer(k):
         return lax.rem(y + k, ny)
 
-    def z_peer(k):
-        return lax.rem(z + k, nz)
+    upper = z // 2
+    mirrored = z * (1 - upper) + (3 - z) * upper
+    z_order = [z]
+    if nz == 4:
+        for near in (1 - mirrored, 2, 3):
+            z_order.append(near * (1 - upper) + (3 - near) * upper)
 
     here = place(x, y, z, core)
     sibling = place(x, y, z, 1 - core)
+    above = place(x, y, lax.rem(z + 1, nz), core)
+    below = place(x, y, lax.rem(z + nz - 1, nz), core)
     x_places = [place(x_peer(k), y, z, core) for k in range(1, nx)]
     y_places = [place(x, y_peer(k), z, core) for k in range(1, ny)]
-    z_places = [place(x, y, z_peer(k), core) for k in range(1, nz)]
-    partners = x_places + y_places + z_places + [sibling]
+    partners = x_places + y_places + [sibling]
+    if nz == 4:
+        partners += [above, below]
 
     barrier = pltpu.get_barrier_semaphore()
     for partner in partners:
@@ -57,44 +66,69 @@
 
     sends = []
 
-    def window(origin, part):
-        return all_ref.at[pl.ds(index(origin) * rows + part * half, half)]
-
-    def send(origin, part, target, own=False):
-        source = own_ref.at[pl.ds(part * half, half)] if own else window(origin, part)
-        copy = pltpu.make_async_remote_copy(
-            src_ref=source,
-            dst_ref=window(origin, part),
-            send_sem=send_sem.at[len(sends)],
-            recv_sem=recv_sem.at[index(origin) * 2 + part],
-            device_id=target,
-            device_id_type=MESH,
-        )
+    def windows(origin, part, own=False):
+        which = index(origin)
+        target = all_ref.at[pl.ds(which * rows + part * half, half)]
+        source = own_ref.at[pl.ds(part * half, half)] if own else target
+        refs = [(source, target, recv_sem.at[which * 3 + part])]
+        if part == 0:
+            codes = all_codes_ref.at[which]
+            refs.append((own_codes_ref.at[0] if own else codes, codes, recv_sem.at[which * 3 + 2]))
+        return refs
+
+    def send(origin, part, target, own=False, condition=None):
+        copies = []
+        for source, destination, semaphore in windows(origin, part, own):
+            copies.append(
+                pltpu.make_async_remote_copy(
+                    src_ref=source,
+                    dst_ref=destination,
+                    send_sem=send_sem.at[len(sends)],
+                    recv_sem=semaphore,
+                    device_id=target,
+                    device_id_type=MESH,
+                )
+            )
+            sends.append((copies[-1], condition))
+
+        def start():
+            for copy in copies:
+                copy.start()
+
+        if condition is None:
+            start()
+        else:
+            pl.when(condition)(start)
+
+    def arrived(origin, part):
+        for _, target, semaphore in windows(origin, part):
+            pltpu.make_async_copy(target, target, semaphore).wait()
+
+    keep = [
+        pltpu.make_async_copy(
+            own_ref, all_ref.at[pl.ds(index(here) * rows, rows)], local_sem.at[0]
+        ),
+        pltpu.make_async_copy(own_codes_ref.at[0], all_codes_ref.at[index(here)], local_sem.at[1]),
+    ]
+    for copy in keep:
         copy.start()
-        sends.append(copy)
-
-    def arrived(origin, part):
-        pltpu.make_async_copy(
-            window(origin, part), window(origin, part), recv_sem.at[index(origin) * 2 + part]
-        ).wait()
-
-    keep = pltpu.make_async_copy(own_ref, all_ref.at[pl.ds(index(here) * rows, rows)], local_sem)
-    keep.start()
 
     def first(k):
-        origin = place(x, y, z_peer(k), core)
-        if k > 0:
+        origin = place(x, y, z_order[k], core)
+        own = k == 0
+        if not own:
             for part in range(2):
                 arrived(origin, part)
-        own = k == 0
+        if nz == 4:
+            going_up = z < 3 if own else (z_order[k] < z) & (z < 3)
+            going_down = z > 0 if own else (z_order[k] > z) & (z > 0)
+            for part in range(2):
+                send(origin, part, above, own, going_up)
+                send(origin, part, below, own, going_down)
         for target in x_places:
             send(origin, 0, target, own)
         for target in y_places:
             send(origin, 1, target, own)
-        if own:
-            for target in z_places:
-                for part in range(2):
-                    send(origin, part, target, own)
         for target in x_places:
             send(origin, 1, target, own)
         for target in y_places:
@@ -104,13 +138,13 @@
 
     def second(k):
         for n in range(1, nx):
-            origin = place(x_peer(n), y, z_peer(k), core)
+            origin = place(x_peer(n), y, z_order[k], core)
             arrived(origin, 0)
             for target in y_places:
                 send(origin, 0, target)
             send(origin, 0, sibling)
         for n in range(1, ny):
-            origin = place(x, y_peer(n), z_peer(k), core)
+            origin = place(x, y_peer(n), z_order[k], core)
             arrived(origin, 1)
             for target in x_places:
                 send(origin, 1, target)
@@ -118,16 +152,16 @@
 
     def third(k):
         for n in range(1, ny):
-            origin = place(x, y_peer(n), z_peer(k), core)
+            origin = place(x, y_peer(n), z_order[k], core)
             arrived(origin, 0)
             send(origin, 0, sibling)
         for n in range(1, nx):
-            origin = place(x_peer(n), y, z_peer(k), core)
+            origin = place(x_peer(n), y, z_order[k], core)
             arrived(origin, 1)
             send(origin, 1, sibling)
         for n in range(1, nx):
             for m in range(1, ny):
-                origin = place(x_peer(n), y_peer(m), z_peer(k), core)
+                origin = place(x_peer(n), y_peer(m), z_order[k], core)
                 for part in range(2):
                     arrived(origin, part)
                     send(origin, part, sibling)
@@ -143,35 +177,43 @@
     for n in range(nx):
         for m in range(ny):
             for k in range(nz):
-                origin = place(x_peer(n), y_peer(m), z_peer(k), 1 - core)
+                origin = place(x_peer(n), y_peer(m), z_order[k], 1 - core)
                 for part in range(2):
                     arrived(origin, part)
-    keep.wait()
-    for copy in sends:
-        copy.wait_send()
+    for copy in keep:
+        copy.wait()
+    for copy, condition in sends:
+        if condition is None:
+            copy.wait_send()
+        else:
+            pl.when(condition)(copy.wait_send)
 
 
 def send_count(sizes):
     nx, ny, nz = sizes
-    plane = 2 * (nx - 1) + 2 * (ny - 1) + 2 * (nx - 1) * (ny - 1)
-    return nz * plane + 2 * (nz - 1) + 2 * nx * ny * nz
-
-
-def gather_rows(own, sizes, total):
-    shape = (total,) + own.shape[1:]
+    plane = (nx - 1) + (ny - 1) + (nx - 1) * (ny - 1)
+    line = 2 * nz if nz > 1 else 0
+    return 3 * (nz * plane + line + nx * ny * nz)
+
+
+def gather_rows(own, own_codes, sizes, total):
+    devices = total // own.shape[0]
     return pl.pallas_call(
         functools.partial(gather_kernel, sizes),
-        out_shape=jax.ShapeDtypeStruct(shape, own.dtype),
-        in_specs=[pl.BlockSpec(memory_space=pl.ANY)],
-        out_specs=pl.BlockSpec(memory_space=pl.ANY),
+        out_shape=(
+            jax.ShapeDtypeStruct((total,) + own.shape[1:], own.dtype),
+            jax.ShapeDtypeStruct((devices,) + own_codes.shape[1:], own_codes.dtype),
+        ),
+        in_specs=[pl.BlockSpec(memory_space=pl.ANY)] * 2,
+        out_specs=[pl.BlockSpec(memory_space=pl.ANY)] * 2,
         scratch_shapes=[
             pltpu.SemaphoreType.DMA((send_count(sizes),)),
-            pltpu.SemaphoreType.DMA((2 * total // own.shape[0],)),
-            pltpu.SemaphoreType.DMA,
+            pltpu.SemaphoreType.DMA((3 * devices,)),
+            pltpu.SemaphoreType.DMA((2,)),
         ],
         compiler_params=pltpu.CompilerParams(collective_id=0, has_side_effects=True),
         name="gather_rows",
-    )(own)
+    )(own, own_codes)
 
 
 def stored_tiles():
@@ -318,9 +360,6 @@
     slot_here = col_here * SLOTS // col_count
     device = row_here * col_count + col_here
 
-    codes = lax.all_gather(block_cols * 2 + block_present, ("row", "col"), axis=0, tiled=True)
-    all_cols = codes // 2
-
     slots = jnp.array([[sent_slot(u, k) for k in range(SENT)] for u in range(SLOTS)], jnp.int32)
     range_here = device * per_device // range_width
     mine = slots[range_here]
@@ -329,7 +368,10 @@
     ]
     parts[-1] = jnp.where(range_here >= SLOTS // 2, jnp.swapaxes(parts[-1], 1, 2), parts[-1])
     own = jnp.stack(parts, axis=1)
-    gathered = gather_rows(own, sizes, block_total)
+    own_codes = (block_cols * 2 + block_present)[None]
+    gathered, codes = gather_rows(own, own_codes, sizes, block_total)
+    codes = codes.reshape(block_total, SLOTS)
+    all_cols = codes // 2
 
     first_row = row_here * panel_rows
     panel = lax.dynamic_slice_in_dim(codes, first_row, panel_rows, 0)

time: 785 us -> 558 us (0.71)
  Pallas kernels: 698 us -> 526 us
  blocking collectives: 56.5 us -> 0 us
    pallas_call x1, Pallas kernels: 524 us -> 351 us  [gather_rows(): pl.pallas_call(functools.partial(gather_kernel, sizes), out_shape=(jax.Sh...]
    all_gather x1 -> x0, blocking collectives: 56.5 us -> none  [body(): lax.all_gather(block_cols * 2 + block_present, ('row', 'col'), axis=0, ti...]
where the time goes in v2:
time: 558 us; the launch traced here: 555 us
  Pallas kernels  526 us (94%)
  local copies, waits for them, and re-layouts  15.8 us (3%)
  between operations  9.81 us (2%)
    pallas_call x1, Pallas kernels, gather_rows(): pl.pallas_call(functools.partial(gather_kernel, sizes), out_shape=(jax.Sh...  351 us
    pallas_call x1, Pallas kernels, sign_rows(): pl.pallas_call(sign_kernel, grid_spec=pltpu.PrefetchScalarGridSpec(num_sc...  175 us

profile of v2, /device:TPU:15, one launch (start us, length us, event | category | flops | bytes accessed | tf_op | source)
XLA Modules:
  0.0 554.6 jit_solution(12508325662283252861)
XLA Ops:
  0.0 0.7 constant_dynamic-slice_fusion.3
  0.7 0.7 fusion.6
  11.0 0.7 add_bitcast_fusion
  11.7 0.7 copy.25.own_codes_ref
  12.4 1.1 dynamic-slice_dynamic-update-slice_fusion.3
  13.5 1.1 dynamic-slice_dynamic-update-slice_fusion.2
  14.6 2.1 dynamic-slice_bitcast_fusion
  16.7 1.3 copy.24
  18.0 1.1 dynamic-slice_dynamic-update-slice_fusion
  19.2 1.3 bitcast_dynamic-update-slice_fusion.own_ref
  20.4 0.0 copy-start
  20.5 1.5 copy-done
  21.9 351.3 %gather_rows.1 = (bf16[512,5,128,128]{3,2,1,0:T(8,128)(2,1)}, s32[32,16,8]{2,1,0:T(8,128)}) custom-call(bf16[16,5,128,128]{3,2,1,0:T(8,128)(2,1)} %copy-done, s32[1,16,8]{2,1,0:T(8,128)} %copy.25.own_codes_ref), custom_call_target="tpu_custom_call" | custom-call | tf_op jit(solution)/shard_map/gather_rows/pallas_call | solution.py:201
  373.3 0.9 constant_dynamic-slice_fusion.2
  374.3 0.1 copy.28
  374.4 0.1 reshape.41
  374.5 0.1 copy.39
  374.6 0.1 reshape.36.present_ref
  374.7 0.1 copy.27
  374.8 0.1 reshape.35.cols_ref
  374.9 1.1 add_select_fusion
  376.0 2.8 gather_fusion
  378.8 0.2 copy.29
  379.4 0.1 stack.79
  379.5 0.3 copy.38
  379.8 0.3 reshape.38.flags_ref
  380.1 174.5 %sign_rows.1 = bf16[128,1,128,128]{3,2,1,0:T(8,128)(2,1)} custom-call(s32[1024]{0:T(1024)S(1)} %reshape.35.cols_ref, s32[5120]{0:T(1024)S(1)} %reshape.38.flags_ref, s32[1024]{0:T(1024)S(1)} %reshape.36.present_ref, s32[128]{0:T(128)S(1)} %and_select_fusion.1.home_ref, s32[128]{0:T(128)S(1)} %fusion.4.live_ref, s32[1]{0:T(128)} %bitcast.61.slot_ref, ...), custom_call_target="tpu_custom_call" | custom-call | flops 42949672960 | bytes 167772160 | tf_op jit(solution)/shard_map/sign_rows/pallas_call | solution.py:327
  (27 shorter events, 0.5 us)
Async XLA Ops:
  20.4 1.5 copy-start

commit v3 on v2

--- a/solution.py
+++ b/solution.py
@@ -27,7 +27,9 @@
     y, core = row // 2, row % 2
     z, x = col // nx, col % nx
     rows = own_ref.shape[0]
-    half = rows // 2
+    last = rows // 4
+    half = (rows - last) // 2
+    starts, lengths = (0, half, rows - last), (half, rows - last - half, last)
     col_count = nx * nz
 
     def place(px, py, pz, pcore):
@@ -68,12 +70,12 @@
 
     def windows(origin, part, own=False):
         which = index(origin)
-        target = all_ref.at[pl.ds(which * rows + part * half, half)]
-        source = own_ref.at[pl.ds(part * half, half)] if own else target
-        refs = [(source, target, recv_sem.at[which * 3 + part])]
+        target = all_ref.at[pl.ds(which * rows + starts[part], lengths[part])]
+        source = own_ref.at[pl.ds(starts[part], lengths[part])] if own else target
+        refs = [(source, target, recv_sem.at[which * 4 + part])]
         if part == 0:
             codes = all_codes_ref.at[which]
-            refs.append((own_codes_ref.at[0] if own else codes, codes, recv_sem.at[which * 3 + 2]))
+            refs.append((own_codes_ref.at[0] if own else codes, codes, recv_sem.at[which * 4 + 3]))
         return refs
 
     def send(origin, part, target, own=False, condition=None):
@@ -166,19 +168,62 @@
                     arrived(origin, part)
                     send(origin, part, sibling)
 
+    def along(origin, k, own=False):
+        if nz == 4:
+            going_up = z < 3 if k == 0 else (z_order[k] < z) & (z < 3)
+            going_down = z > 0 if k == 0 else (z_order[k] > z) & (z > 0)
+            send(origin, 2, above, own, going_up)
+            send(origin, 2, below, own, going_down)
+        send(origin, 2, sibling, own)
+
+    def plane_own():
+        for target in x_places + y_places:
+            send(here, 2, target, True)
+        along(here, 0, True)
+
+    def plane_x():
+        for n in range(1, nx):
+            origin = place(x_peer(n), y, z, core)
+            arrived(origin, 2)
+            for target in y_places:
+                send(origin, 2, target)
+            along(origin, 0)
+
+    def plane_y():
+        for m in range(1, ny):
+            for n in range(nx):
+                origin = place(x_peer(n), y_peer(m), z, core)
+                arrived(origin, 2)
+                along(origin, 0)
+
+    def line(k):
+        for m in range(ny):
+            for n in range(nx):
+                origin = place(x_peer(n), y_peer(m), z_order[k], core)
+                arrived(origin, 2)
+                along(origin, k)
+
     for k in range(nz + 2):
         if k < nz:
             first(k)
+        if k == 0:
+            plane_own()
+        if k == 1:
+            plane_x()
         if 0 <= k - 1 < nz:
             second(k - 1)
+        if k == 1:
+            plane_y()
         if 0 <= k - 2 < nz:
             third(k - 2)
+        if 1 <= k - 2 < nz:
+            line(k - 2)
 
     for n in range(nx):
         for m in range(ny):
             for k in range(nz):
                 origin = place(x_peer(n), y_peer(m), z_order[k], 1 - core)
-                for part in range(2):
+                for part in range(3):
                     arrived(origin, part)
     for copy in keep:
         copy.wait()
@@ -192,8 +237,8 @@
 def send_count(sizes):
     nx, ny, nz = sizes
     plane = (nx - 1) + (ny - 1) + (nx - 1) * (ny - 1)
-    line = 2 * nz if nz > 1 else 0
-    return 3 * (nz * plane + line + nx * ny * nz)
+    line = 2 * nz * (3 + nx * ny) if nz > 1 else 0
+    return 3 * nz * plane + line + 4 * nx * ny * nz + plane
 
 
 def gather_rows(own, own_codes, sizes, total):
@@ -208,7 +253,7 @@
         out_specs=[pl.BlockSpec(memory_space=pl.ANY)] * 2,
         scratch_shapes=[
             pltpu.SemaphoreType.DMA((send_count(sizes),)),
-            pltpu.SemaphoreType.DMA((3 * devices,)),
+            pltpu.SemaphoreType.DMA((4 * devices,)),
             pltpu.SemaphoreType.DMA((2,)),
         ],
         compiler_params=pltpu.CompilerParams(collective_id=0, has_side_effects=True),
@@ -270,25 +315,20 @@
                     kept, block, jnp.zeros_like(block)
                 )
 
-    def plain(left, n):
-        return jnp.dot(left, tile_ref[n], preferred_element_type=jnp.float32)
-
-    def turned(left, n):
-        return lax.dot_general(
-            left, tile_ref[n], (((1,), (1,)), ((), ())), preferred_element_type=jnp.float32
+    def column(left, t):
+        plain = [(first, n) for n, (first, second, _) in enumerate(TILES) if second == t]
+        turned = [(second, n) for n, (first, second, _) in enumerate(TILES) if first == t != second]
+        total = jnp.dot(
+            jnp.concatenate([left(p) for p, _ in plain], axis=1),
+            jnp.concatenate([tile_ref[n] for _, n in plain], axis=0),
+            preferred_element_type=jnp.float32,
         )
-
-    def column(left, t):
-        total = None
-        for n, (first, second, _) in enumerate(TILES):
-            term = None
-            if second == t:
-                term = plain(left(first), n)
-            elif first == t:
-                term = turned(left(second), n)
-            if term is not None:
-                total = term if total is None else total + term
-        return total
+        return total + lax.dot_general(
+            jnp.concatenate([left(p) for p, _ in turned], axis=1),
+            jnp.concatenate([tile_ref[n] for _, n in turned], axis=1),
+            (((1,), (1,)), ((), ())),
+            preferred_element_type=jnp.float32,
+        )
 
     def left_tile(t):
         return jnp.concatenate([left_ref[2 * t], left_ref[2 * t + 1]], axis=1)

time: 558 us -> 584 us (1.047); the launches traced: 555 us -> 573 us
  Pallas kernels: 526 us -> 545 us
    pallas_call x1, Pallas kernels: 351 us -> 376 us  [gather_rows(): pl.pallas_call(functools.partial(gather_kernel, sizes), out_shape=(jax.Sh...]
where the time goes in v3:
time: 584 us; the launch traced here: 573 us
  Pallas kernels  545 us (93%)
  local copies, waits for them, and re-layouts  15.8 us (3%)
  between operations  9.81 us (2%)
    pallas_call x1, Pallas kernels, gather_rows(): pl.pallas_call(functools.partial(gather_kernel, sizes), out_shape=(jax.Sh...  376 us
    pallas_call x1, Pallas kernels, sign_rows(): pl.pallas_call(sign_kernel, grid_spec=pltpu.PrefetchScalarGridSpec(num_sc...  169 us

profile of v3, /device:TPU:15, one launch (start us, length us, event | category | flops | bytes accessed | tf_op | source)
XLA Modules:
  0.0 573.4 jit_solution(2234868632672816077)
XLA Ops:
  0.0 0.7 constant_dynamic-slice_fusion.3
  0.7 0.7 fusion.6
  11.0 0.7 add_bitcast_fusion
  11.7 0.7 copy.25.own_codes_ref
  12.4 1.1 dynamic-slice_dynamic-update-slice_fusion.3
  13.5 1.1 dynamic-slice_dynamic-update-slice_fusion.2
  14.6 2.1 dynamic-slice_bitcast_fusion
  16.7 1.3 copy.24
  18.0 1.1 dynamic-slice_dynamic-update-slice_fusion
  19.2 1.3 bitcast_dynamic-update-slice_fusion.own_ref
  20.4 0.0 copy-start
  20.5 1.5 copy-done
  21.9 375.9 %gather_rows.1 = (bf16[512,5,128,128]{3,2,1,0:T(8,128)(2,1)}, s32[32,16,8]{2,1,0:T(8,128)}) custom-call(bf16[16,5,128,128]{3,2,1,0:T(8,128)(2,1)} %copy-done, s32[1,16,8]{2,1,0:T(8,128)} %copy.25.own_codes_ref), custom_call_target="tpu_custom_call" | custom-call | tf_op jit(solution)/shard_map/gather_rows/pallas_call | solution.py:246
  397.8 0.9 constant_dynamic-slice_fusion.2
  398.8 0.1 copy.28
  398.9 0.1 reshape.41
  399.0 0.1 copy.39
  399.1 0.1 reshape.36.present_ref
  399.2 0.1 copy.27
  399.3 0.1 reshape.35.cols_ref
  399.4 1.1 add_select_fusion
  400.5 2.8 gather_fusion
  403.3 0.2 copy.29
  404.0 0.1 stack.79
  404.0 0.3 copy.38
  404.3 0.3 reshape.38.flags_ref
  404.6 168.8 %sign_rows.1 = bf16[128,1,128,128]{3,2,1,0:T(8,128)(2,1)} custom-call(s32[1024]{0:T(1024)S(1)} %reshape.35.cols_ref, s32[5120]{0:T(1024)S(1)} %reshape.38.flags_ref, s32[1024]{0:T(1024)S(1)} %reshape.36.present_ref, s32[128]{0:T(128)S(1)} %and_select_fusion.1.home_ref, s32[128]{0:T(128)S(1)} %fusion.4.live_ref, s32[1]{0:T(128)} %bitcast.61.slot_ref, ...), custom_call_target="tpu_custom_call" | custom-call | flops 42949672960 | bytes 167772160 | tf_op jit(solution)/shard_map/sign_rows/pallas_call | solution.py:367
  (27 shorter events, 0.5 us)
Async XLA Ops:
  20.4 1.5 copy-start
